TPU v7x, 32 devices: a whole 2x2x4 slice. The times are simulated.
32 devices in a mesh: dp: 8 (over y, x, core), tensor: 4 (over z).
Axes of the slice: x: 2, y: 2, z: 4, core: 2. Of those that a mesh axis runs over, the one named last changes fastest.
Arguments:
- kept_input: bfloat16 [768, 4096], P(('dp', 'tensor')), may hold values from -6 to 6
- kept_grad: bfloat16 [768, 4096], P(('dp', 'tensor')), may hold values from -6 to 6
- up_weight_t: bfloat16 [8256, 4096], P('tensor'), may hold values from -0.09375 to 0.09375
- up_bias: bfloat16 [8256], P('tensor'), may hold values from -4 to 4
- down_weight: bfloat16 [8256, 4096], P('tensor'), may hold values from -0.0625 to 0.0625
- kept_count: int32 [32], P(('dp', 'tensor')), may hold values from 8 to 24, as said below
Outputs:
- grad_kept: bfloat16 [768, 4096], P(('dp', 'tensor'))
Inputs may be any that keep to these rules, and one draw needn't show every extreme that they name: `kept_count`: every block keeps at least 8 and at most 24 of its 24 slots, some block exactly 24. Among the 8 blocks of one tensor index taken in order of g, the blocks before block g keep g * 16 + e tokens together with e between -4 and 4, and e is 0 for g = 0 and for g = 8 (all 8 blocks together keep exactly 128 tokens).
All inputs are finite; a program needn't handle non-finite values.
Results may differ from a plain program's by a relative error of at most 0.014.
Values may be sent and summed in bfloat16 or wider, within the bound.
A program may use at most 64 MiB of HBM per device.

v0:
```python
import jax
import jax.numpy as jnp
from jax import lax
from jax.sharding import PartitionSpec as P

BAL = 16


INV_SQRT_TWO = 0.7071067811865476
INV_SQRT_TWO_PI = 0.3989422804014327


def prefix(shard, axis, combine, identity):
    length, index = (lax.axis_size(axis), lax.axis_index(axis))
    everything = lax.all_gather(shard, axis)
    start = jnp.broadcast_to(jnp.asarray(identity, shard.dtype), shard.shape)

    def lap(k, before):
        reached = k < index
        new = combine(before, everything[k])
        return jnp.where(reached, new, before)

    return lax.fori_loop(0, length, lap, start)


def padded(block, sides, width):
    for axis, dim in sides:
        count = lax.axis_size(axis)
        forward = [(i, i + 1) for i in range(count - 1)]
        backward = [(target, source) for source, target in forward]
        low = lax.ppermute(
            lax.slice_in_dim(block, block.shape[dim] - width, None, axis=dim), axis, forward
        )
        high = lax.ppermute(lax.slice_in_dim(block, 0, width, axis=dim), axis, backward)
        block = jnp.concatenate([low, block, high], axis=dim)
    return block


def gelu_slope(values):
    return (
        0.5 * (1.0 + lax.erf(values * INV_SQRT_TWO))
        + values * jnp.exp(-0.5 * values * values) * INV_SQRT_TWO_PI
    )


def add_counts(earlier, later):
    return earlier + later


def ffn_rows(stacked, up_weight_t, up_bias, down_weight):
    contract = (((1,), (1,)), ((), ()))
    bias_wide = up_bias.astype(jnp.float32)
    piece_rows = lax.all_gather(stacked, "tensor", axis=0, tiled=True)
    inputs = piece_rows[:, 0]
    out_grads = piece_rows[:, 1]
    preact = (
        lax.dot_general(inputs, up_weight_t, contract, preferred_element_type=jnp.float32)
        + bias_wide
    )
    down_grad = lax.dot_general(
        out_grads, down_weight, contract, preferred_element_type=jnp.float32
    )
    pre_grad = (gelu_slope(preact) * down_grad).astype(jnp.bfloat16)
    partials = jnp.dot(pre_grad, up_weight_t, preferred_element_type=jnp.float32)
    return lax.psum_scatter(
        partials.astype(jnp.bfloat16), "tensor", scatter_dimension=0, tiled=True
    )


def body(kept_input, kept_grad, up_weight_t, up_bias, down_weight, kept_count):
    kmax = kept_input.shape[0]
    count_here = kept_count[0]
    entries = jnp.arange(kmax, dtype=jnp.int32)
    usable = entries < count_here
    stacked = jnp.stack((kept_input, kept_grad), axis=1)
    stacked = jnp.where(usable[:, None, None], stacked, jnp.zeros_like(stacked))
    halo_width = BAL // 4
    spots = BAL + 2 * halo_width
    first_slot = prefix(count_here, "dp", add_counts, jnp.int32(0))
    excess = first_slot - lax.axis_index("dp") * BAL
    target = excess + entries + halo_width
    placing = (target[None, :] == jnp.arange(spots, dtype=jnp.int32)[:, None]) & usable[None, :]
    placing_mat = placing.astype(jnp.bfloat16)
    outgoing = jnp.einsum(
        "sk,kcd->scd", placing_mat, stacked, preferred_element_type=jnp.float32
    ).astype(jnp.bfloat16)
    widened = padded(outgoing, (("dp", 0),), halo_width)
    owned = outgoing[halo_width : halo_width + BAL].astype(jnp.float32)
    owned = owned.at[:halo_width].add(widened[:halo_width].astype(jnp.float32))
    owned = owned.at[BAL - halo_width :].add(
        widened[widened.shape[0] - halo_width :].astype(jnp.float32)
    )
    branch = ffn_rows(owned.astype(jnp.bfloat16), up_weight_t, up_bias, down_weight)
    returned = padded(branch, (("dp", 0),), halo_width)
    own_branch = jnp.einsum(
        "sk,sd->kd", placing_mat, returned, preferred_element_type=jnp.float32
    ).astype(jnp.bfloat16)
    summed = kept_grad.astype(jnp.float32) + own_branch.astype(jnp.float32)
    return jnp.where(usable[:, None], summed, jnp.float32(0.0)).astype(jnp.bfloat16)


def solution(mesh):
    placed = (
        P(("dp", "tensor"), None),
        P(("dp", "tensor"), None),
        P("tensor", None),
        P("tensor"),
        P("tensor", None),
        P(("dp", "tensor")),
    )
    return jax.shard_map(
        body, mesh=mesh, in_specs=placed, out_specs=P(("dp", "tensor"), None), check_vma=False
    )
```

profile of v0, /device:TPU:1, one launch (start us, length us, event | category | flops | bytes accessed | tf_op | source)
XLA Modules:
  0.0 135.0 jit_solution(1891184840131125109)
XLA Ops:
  6.5 0.0 all-gather.2.cloned.1.call-start
  7.2 1.3 dynamic-slice.16
  8.5 0.7 dynamic-update-slice.6
  9.2 7.3 %all-reduce = s32[8]{0:T(128)S(1)} all-reduce(s32[8]{0:T(128)S(1)} %dynamic-update-slice.6), channel_id=1, replica_groups=mesh['dp'=8,'tensor'=4] {'dp'}, use_global_device_ids=true, to_apply=%add | all-reduce | flops 8 | bytes 64
  16.5 10.4 %while.15 = (s32[]{:T(128)}, s32[]{:T(128)}, s32[]{:T(128)}, s32[8]{0:T(128)S(1)}, s32[]{:T(128)}) while((s32[]{:T(128)}, s32[]{:T(128)}, s32[]{:T(128)}, s32[8]{0:T(128)S(1)}, s32[]{:T(128)}) %tuple.38), condition=%wide.region_1.2_spmd, body=%wide.region_0.1_spmd.sunk | while | flops 5 | bytes 115 | solution.py:23
  16.5 0.6 dynamic_slice.8
  17.8 0.7 dynamic_slice.8
  19.1 0.7 dynamic_slice.8
  20.5 0.7 dynamic_slice.8
  21.8 0.7 dynamic_slice.8
  23.1 0.7 dynamic_slice.8
  24.4 0.7 dynamic_slice.8
  25.7 0.7 dynamic_slice.8
  27.0 1.3 convolution_convert_fusion.1
  28.3 0.1 fusion.46
  28.4 4.1 %collective-permute-start.1 = (bf16[4,2,4096]{2,0,1:T(4,128)(2,1)S(1)}, bf16[4,2,4096]{2,0,1:T(4,128)(2,1)S(1)}, u32[]{:S(2)}, u32[]{:S(2)}) collective-permute-start(bf16[4,2,4096]{2,0,1:T(4,128)(2,1)S(1)} %get-tuple-element.117), channel_id=1, source_target_pairs={{4,0},{8,4},{12,8},{16,12},{20,16},{24,20},{28,24},{5,1},{9,5},{13... | collective-permute-start | bytes 196616 | tf_op jit(solution)/shard_map/ppermute | solution.py:34
  32.5 2.4 %collective-permute-start = (bf16[4,2,4096]{2,0,1:T(4,128)(2,1)S(1)}, bf16[4,2,4096]{2,0,1:T(4,128)(2,1)S(1)}, u32[]{:S(2)}, u32[]{:S(2)}) collective-permute-start(bf16[4,2,4096]{2,0,1:T(4,128)(2,1)S(1)} %get-tuple-element.118), channel_id=1, source_target_pairs={{0,4},{4,8},{8,12},{12,16},{16,20},{20,24},{24,28},{1,5},{5,9},{9,... | collective-permute-start | bytes 196616 | tf_op jit(solution)/shard_map/ppermute | solution.py:31
  34.9 0.1 slice_convert_fusion
  35.0 1.2 collective-permute-done
  36.2 0.1 fusion.29
  36.3 0.0 collective-permute-done.1
  36.3 0.1 fusion.28
  36.4 0.7 convert_element_type.42
  37.1 0.0 all-gather.2.cloned.1.call-update
  37.1 0.0 reduce-scatter.2.cloned.1.call-start
  37.2 0.7 convert_element_type.43
  37.9 28.6 %all-gather.2.cloned.1.call-done = bf16[64,2,4096]{2,0,1:T(8,128)(2,1)} async-done(((bf16[16,2,4096]{2,0,1:T(8,128)(2,1)}), bf16[64,2,4096]{2,0,1:T(8,128)(2,1)}) %all-gather.2.cloned.1.call-update) | async-done | bytes 1048592 | tf_op jit(solution)/shard_map/all_gather | solution.py:53
  66.5 0.0 copy-start
  66.5 11.4 %convolution_add_fusion = f32[64,2064]{1,0:T(8,128)S(1)} fusion(bf16[2064,4096]{1,0:T(8,128)(2,1)} %param.14, bf16[64,2,4096]{2,0,1:T(8,128)(2,1)} %all-gather.2.cloned.1.call-done, f32[2064]{0:T(1024)S(1)} %convert_element_type.43), kind=kOutput, calls=%fused_computation.8 | convolution fusion | flops 1082262528 | bytes 17969216 | tf_op jit(solution)/shard_map/dot_general | solution.py:57
  77.9 0.0 copy-done
  77.9 0.0 copy-start.1
  77.9 17.2 %convolution_convert_fusion = bf16[64,4096]{1,0:T(8,128)(2,1)} fusion(bf16[2064,4096]{1,0:T(8,128)(2,1)} %param.14, bf16[2064,4096]{1,0:T(8,128)(2,1)} %param.16, f32[64,2064]{1,0:T(8,128)S(1)} %convolution_add_fusion, bf16[64,2,4096]{2,0,1:T(8,128)(2,1)S(1)} %copy-done), kind=kOutput, calls=%fused_computation | convolution fusion | flops 2165843968 | bytes 35422208 | tf_op jit(solution)/shard_map/dot_general | solution.py:64
  95.1 0.0 reduce-scatter.2.cloned.1.call-update
  95.1 19.7 %reduce-scatter.2.cloned.1.call-done = bf16[16,4096]{1,0:T(8,128)(2,1)} async-done(((bf16[64,4096]{1,0:T(8,128)(2,1)}), bf16[16,4096]{1,0:T(8,128)(2,1)}) %reduce-scatter.2.cloned.1.call-update) | async-done | bytes 131088 | tf_op jit(solution)/shard_map/reduce_scatter | solution.py:65
  114.9 0.9 fusion.47
  115.8 5.3 %collective-permute-start.2 = (bf16[4,4096]{1,0:T(4,128)(2,1)S(1)}, bf16[4,4096]{1,0:T(4,128)(2,1)S(1)}, u32[]{:S(2)}, u32[]{:S(2)}) collective-permute-start(bf16[4,4096]{1,0:T(4,128)(2,1)S(1)} %get-tuple-element.119), channel_id=1, source_target_pairs={{0,4},{4,8},{8,12},{12,16},{16,20},{20,24},{24,28},{1,5},{5,9},{9,... | collective-permute-start | bytes 98312 | tf_op jit(solution)/shard_map/ppermute | solution.py:31
  121.1 1.9 %collective-permute-start.3 = (bf16[4,4096]{1,0:T(4,128)(2,1)S(1)}, bf16[4,4096]{1,0:T(4,128)(2,1)S(1)}, u32[]{:S(2)}, u32[]{:S(2)}) collective-permute-start(bf16[4,4096]{1,0:T(4,128)(2,1)S(1)} %get-tuple-element.120), channel_id=1, source_target_pairs={{4,0},{8,4},{12,8},{16,12},{20,16},{24,20},{28,24},{5,1},{9,5},{13... | collective-permute-start | bytes 98312 | tf_op jit(solution)/shard_map/ppermute | solution.py:34
  123.0 0.0 collective-permute-done.2
  123.0 3.3 %collective-permute-done.3 = bf16[4,4096]{1,0:T(4,128)(2,1)S(1)} collective-permute-done((bf16[4,4096]{1,0:T(4,128)(2,1)S(1)}, bf16[4,4096]{1,0:T(4,128)(2,1)S(1)}, u32[]{:S(2)}, u32[]{:S(2)}) %collective-permute-start.3) | collective-permute-done | bytes 32800 | tf_op jit(solution)/shard_map/ppermute | solution.py:34
  126.3 0.0 copy-done.1
  126.3 1.8 %fusion.3 = bf16[24,4096]{1,0:T(8,128)(2,1)} fusion(bf16[24,4096]{1,0:T(8,128)(2,1)S(1)} %copy-done.1, bf16[4,4096]{1,0:T(4,128)(2,1)S(1)} %collective-permute-done.3, bf16[16,4096]{1,0:T(8,128)(2,1)} %reduce-scatter.2.cloned.1.call-done, bf16[4,4096]{1,0:T(4,128)(2,1)S(1)} %collective-permute-done.2, pred[24]{0:T(512)(128)(4,1)S(1)} %iota_compare_fusion.1, ...), kind=kOutput, calls=%fused_computation.6 | convolution fusion | flops 5899392 | bytes 589944 | tf_op jit(solution)/shard_map/sk,sd->kd/dot_general | solution.py:95
  (3 shorter events, 0.0 us)
Async XLA Ops:
  6.5 60.0 %all-gather.2.cloned.1.call-start = ((), (), s32[]{:S(2)}) async-start(), calls=%async_computation.1 | async-start | bytes 1310720 | tf_op jit(solution)/shard_map/all_gather | solution.py:53
  28.4 7.9 %collective-permute-start.1 = (bf16[4,2,4096]{2,0,1:T(4,128)(2,1)S(1)}, bf16[4,2,4096]{2,0,1:T(4,128)(2,1)S(1)}, u32[]{:S(2)}, u32[]{:S(2)}) collective-permute-start(bf16[4,2,4096]{2,0,1:T(4,128)(2,1)S(1)} %get-tuple-element.117), channel_id=1, source_target_pairs={{4,0},{8,4},{12,8},{16,12},{20,16},{24,20},{28,24},{5,1},{9,5},{13... | collective-permute-start | bytes 196616 | tf_op jit(solution)/shard_map/ppermute | solution.py:34
  32.5 3.7 %collective-permute-start = (bf16[4,2,4096]{2,0,1:T(4,128)(2,1)S(1)}, bf16[4,2,4096]{2,0,1:T(4,128)(2,1)S(1)}, u32[]{:S(2)}, u32[]{:S(2)}) collective-permute-start(bf16[4,2,4096]{2,0,1:T(4,128)(2,1)S(1)} %get-tuple-element.118), channel_id=1, source_target_pairs={{0,4},{4,8},{8,12},{12,16},{16,20},{20,24},{24,28},{1,5},{5,9},{9,... | collective-permute-start | bytes 196616 | tf_op jit(solution)/shard_map/ppermute | solution.py:31
  37.1 77.7 %reduce-scatter.2.cloned.1.call-start = ((), (), s32[]{:S(2)}) async-start(), calls=%async_computation.2 | async-start | bytes 655360 | tf_op jit(solution)/shard_map/reduce_scatter | solution.py:65
  66.5 11.4 %copy-start = (bf16[64,2,4096]{2,0,1:T(8,128)(2,1)S(1)}, bf16[64,2,4096]{2,0,1:T(8,128)(2,1)}, u32[]{:S(2)}) copy-start(bf16[64,2,4096]{2,0,1:T(8,128)(2,1)} %all-gather.2.cloned.1.call-done) | copy-start | bytes 3145732
  77.9 48.4 %copy-start.1 = (bf16[24,4096]{1,0:T(8,128)(2,1)S(1)}, bf16[24,4096]{1,0:T(8,128)(2,1)}, u32[]{:S(2)}) copy-start(bf16[24,4096]{1,0:T(8,128)(2,1)} %param.13) | copy-start | bytes 589828
  115.8 7.2 %collective-permute-start.2 = (bf16[4,4096]{1,0:T(4,128)(2,1)S(1)}, bf16[4,4096]{1,0:T(4,128)(2,1)S(1)}, u32[]{:S(2)}, u32[]{:S(2)}) collective-permute-start(bf16[4,4096]{1,0:T(4,128)(2,1)S(1)} %get-tuple-element.119), channel_id=1, source_target_pairs={{0,4},{4,8},{8,12},{12,16},{16,20},{20,24},{24,28},{1,5},{5,9},{9,... | collective-permute-start | bytes 98312 | tf_op jit(solution)/shard_map/ppermute | solution.py:31
  121.1 5.2 %collective-permute-start.3 = (bf16[4,4096]{1,0:T(4,128)(2,1)S(1)}, bf16[4,4096]{1,0:T(4,128)(2,1)S(1)}, u32[]{:S(2)}, u32[]{:S(2)}) collective-permute-start(bf16[4,4096]{1,0:T(4,128)(2,1)S(1)} %get-tuple-element.120), channel_id=1, source_target_pairs={{4,0},{8,4},{12,8},{16,12},{20,16},{24,20},{28,24},{5,1},{9,5},{13... | collective-permute-start | bytes 98312 | tf_op jit(solution)/shard_map/ppermute | solution.py:34
Sparse Core Ops, SparseCore 0:
  37.3 29.2 all-gather.1
  95.3 19.5 reduce-scatter.1
where the time goes:
time: 135 us
  waiting for transfers between devices  52.9 us (39%)
  matrix products  31.7 us (23%)
  between operations  14.2 us (11%)
  starting transfers between devices  13.8 us (10%)
  local copies, waits for them, and re-layouts  8.2 us (6%)
  blocking collectives  7.3 us (5%)
  loops' own time  5.22 us (4%)
  other arithmetic  1.65 us (1%)
    all_gather x1, waiting for transfers between devices, ffn_rows(): piece_rows = lax.all_gather(stacked, 'tensor', axis=0, tiled=True)  28.6 us
    reduce_scatter x1, waiting for transfers between devices, ffn_rows(): lax.psum_scatter(partials.astype(jnp.bfloat16), 'tensor', scatter_dimensi...  19.7 us
    dot_general x1, matrix products, ffn_rows(): jnp.dot(pre_grad, up_weight_t, preferred_element_type=jnp.float32)  17.2 us
    dot_general x1, matrix products, ffn_rows(): lax.dot_general(inputs, up_weight_t, contract, preferred_element_type=jnp...  11.4 us
    ppermute x2, starting transfers between devices, padded(): lax.ppermute(lax.slice_in_dim(block, block.shape[dim] - width, None, axis...  7.66 us
    unnamed x1, blocking collectives  7.3 us
    ppermute x2, starting transfers between devices, padded(): lax.ppermute(lax.slice_in_dim(block, 0, width, axis=dim), axis, backward)  6.05 us
    another operation x1, loops' own time, prefix(): return lax.fori_loop(0, length, lap, start)  5.22 us
  transfers between devices with their start and end apart: 6, of which 4 were waited for; matrix products, arithmetic and copies ran while one was open for 1% of the time, Pallas kernels for 0%

commit v1 on v0

--- a/solution.py
+++ b/solution.py
@@ -1,6 +1,10 @@
+import functools
+
 import jax
 import jax.numpy as jnp
 from jax import lax
+from jax.experimental import pallas as pl
+from jax.experimental.pallas import tpu as pltpu
 from jax.sharding import PartitionSpec as P
 
 BAL = 16
@@ -99,15 +103,301 @@
     return jnp.where(usable[:, None], summed, jnp.float32(0.0)).astype(jnp.bfloat16)
 
 
+ROWS = 16
+COLS = 512
+VMEM_LIMIT = 58 * 1024 * 1024
+MESH = pl.DeviceIdType.MESH
+NT = (((1,), (1,)), ((), ()))
+
+
+def one_hot(shape, picked):
+    rows = lax.broadcasted_iota(jnp.int32, shape, 0)
+    cols = lax.broadcasted_iota(jnp.int32, shape, 1)
+    return picked(rows, cols).astype(jnp.float32).astype(jnp.bfloat16)
+
+
+def place(matrix, block):
+    return jnp.dot(matrix, block, preferred_element_type=jnp.float32)
+
+
+def fused_kernel(
+    n_dp, n_t, x_ref, g_ref, count_ref, bias_ref, up_hbm, down_hbm, out_ref,
+    up, down, rows_in, terms, taken, branch, acc_x, acc_g, slopes,
+    count_own, counts, halo_out, halo_in, back_out, back_in,
+    w_sem, count_send, count_recv, halo_send, halo_recv, back_send, back_recv,
+    in_send, in_recv, term_send, term_recv,
+):
+    me = lax.axis_index("dp")
+    t = lax.axis_index("tensor")
+    kmax, width = x_ref.shape
+    chunks = width // COLS
+    halo = BAL // 4
+    groups = ROWS // halo
+    wide = width // groups
+    per_group = wide // COLS
+    left = lax.rem(me + n_dp - 1, n_dp)
+    right = lax.rem(me + 1, n_dp)
+
+    def weight_copies(c):
+        cols = pl.ds(pl.multiple_of(c * COLS, COLS), COLS)
+        return (
+            pltpu.make_async_copy(up_hbm.at[:, cols], up.at[c], w_sem.at[0, c]),
+            pltpu.make_async_copy(down_hbm.at[:, cols], down.at[c], w_sem.at[1, c]),
+        )
+
+    @pl.loop(0, chunks)
+    def _(c):
+        for copy in weight_copies(c):
+            copy.start()
+
+    barrier = pltpu.get_barrier_semaphore()
+    for k in range(1, n_dp):
+        pl.semaphore_signal(
+            barrier, inc=1, device_id={"dp": lax.rem(me + k, n_dp)}, device_id_type=MESH
+        )
+    for k in range(1, n_t):
+        pl.semaphore_signal(
+            barrier, inc=1, device_id={"tensor": lax.rem(t + k, n_t)}, device_id_type=MESH
+        )
+
+    here = count_ref[0]
+    count_own[...] = jnp.full(count_own.shape, here, jnp.int32)
+    for j in range(groups):
+        cols = slice(j * wide, (j + 1) * wide)
+        head = one_hot((ROWS, kmax), lambda r, k: (r // halo == j) & (k == r % halo))
+        tail = one_hot(
+            (ROWS, kmax), lambda r, k: (r // halo == j) & (k == here - halo + r % halo)
+        )
+        for i, ref in enumerate((x_ref, g_ref)):
+            for side, matrix in enumerate((head, tail)):
+                part = place(matrix, ref[:, cols]).astype(jnp.bfloat16)
+                if j == 0:
+                    halo_out[side, i] = part
+                else:
+                    halo_out[side, i] += part
+    pl.semaphore_wait(barrier, n_dp - 1 + n_t - 1)
+
+    def count_copy(k, source):
+        return pltpu.make_async_remote_copy(
+            src_ref=count_own, dst_ref=counts.at[source],
+            send_sem=count_send.at[k - 1], recv_sem=count_recv.at[source],
+            device_id={"dp": lax.rem(me + k, n_dp)}, device_id_type=MESH,
+        )
+
+    def side_copy(side, source, target, send, recv):
+        return pltpu.make_async_remote_copy(
+            src_ref=source.at[side], dst_ref=target.at[1 - side],
+            send_sem=send.at[side], recv_sem=recv.at[1 - side],
+            device_id={"dp": right if side else left}, device_id_type=MESH,
+        )
+
+    for side in range(2):
+        side_copy(side, halo_out, halo_in, halo_send, halo_recv).start()
+    for k in range(1, n_dp):
+        count_copy(k, me).start()
+    for k in range(1, n_dp):
+        count_copy(k, lax.rem(me + n_dp - k, n_dp)).wait_recv()
+    before = jnp.zeros(count_own.shape, jnp.int32)
+    for j in range(n_dp):
+        before = before + jnp.where(j < me, counts[j], 0)
+    excess = (before - me * BAL)[0:1, 0:1]
+    following = excess + here - BAL
+
+    def in_copy(k, c, source):
+        return pltpu.make_async_remote_copy(
+            src_ref=rows_in.at[source, c], dst_ref=rows_in.at[source, c],
+            send_sem=in_send.at[k - 1, c], recv_sem=in_recv.at[source, c],
+            device_id={"tensor": lax.rem(t + k, n_t)}, device_id_type=MESH,
+        )
+
+    own_at = one_hot(
+        (ROWS, kmax), lambda p, k: (k == p - excess) & (k < here)
+    )
+    for side in range(2):
+        side_copy(side, halo_out, halo_in, halo_send, halo_recv).wait_recv()
+    for j in range(groups):
+        cols = slice(j * wide, (j + 1) * wide)
+        from_left = one_hot(
+            (ROWS, ROWS), lambda p, r: (r == j * halo + halo - excess + p) & (p < excess)
+        )
+        from_right = one_hot(
+            (ROWS, ROWS),
+            lambda p, r: (r == j * halo + p - BAL - following) & (p >= BAL + following),
+        )
+        for i, ref in enumerate((x_ref, g_ref)):
+            window = (
+                place(own_at, ref[:, cols])
+                + place(from_left, halo_in[0, i])
+                + place(from_right, halo_in[1, i])
+            ).astype(jnp.bfloat16)
+            for s in range(per_group):
+                rows_in[t, j * per_group + s, i] = window[:, s * COLS : (s + 1) * COLS]
+        for s in range(per_group):
+            for k in range(1, n_t):
+                in_copy(k, j * per_group + s, t).start()
+
+    acc_x[...] = jnp.broadcast_to(bias_ref[...].astype(jnp.float32), acc_x.shape)
+    acc_g[...] = jnp.zeros_like(acc_g)
+
+    @pl.loop(0, chunks)
+    def _(c):
+        for copy in weight_copies(c):
+            copy.wait()
+        for k in range(1, n_t):
+            in_copy(k, c, lax.rem(t + n_t - k, n_t)).wait_recv()
+        x = rows_in[:, c, 0].reshape(n_t * ROWS, COLS)
+        g = rows_in[:, c, 1].reshape(n_t * ROWS, COLS)
+        acc_x[...] += lax.dot_general(x, up[c], NT, preferred_element_type=jnp.float32)
+        acc_g[...] += lax.dot_general(g, down[c], NT, preferred_element_type=jnp.float32)
+
+    slopes[...] = (gelu_slope(acc_x[...]) * acc_g[...]).astype(jnp.bfloat16)
+
+    def term_copy(k, c, source):
+        dest = lax.rem(t + k, n_t)
+        return pltpu.make_async_remote_copy(
+            src_ref=terms.at[c, dest], dst_ref=taken.at[source, c],
+            send_sem=term_send.at[k - 1, c], recv_sem=term_recv.at[source, c],
+            device_id={"tensor": dest}, device_id_type=MESH,
+        )
+
+    @pl.loop(0, chunks)
+    def _(c):
+        term = jnp.dot(slopes[...], up[c], preferred_element_type=jnp.float32)
+        terms[c] = term.astype(jnp.bfloat16).reshape(n_t, ROWS, COLS)
+        for k in range(1, n_t):
+            term_copy(k, c, t).start()
+
+    for c in range(chunks):
+        total = terms[c, t].astype(jnp.float32)
+        for k in range(1, n_t):
+            source = lax.rem(t + n_t - k, n_t)
+            term_copy(k, c, source).wait_recv()
+            total = total + taken[source, c].astype(jnp.float32)
+        branch[:, c * COLS : (c + 1) * COLS] = total.astype(jnp.bfloat16)
+
+    for j in range(groups):
+        cols = slice(j * wide, (j + 1) * wide)
+        head = one_hot((ROWS, ROWS), lambda r, p: (r // halo == j) & (p == r % halo))
+        tail = one_hot(
+            (ROWS, ROWS), lambda r, p: (r // halo == j) & (p == BAL - halo + r % halo)
+        )
+        for side, matrix in enumerate((head, tail)):
+            part = place(matrix, branch[:, cols]).astype(jnp.bfloat16)
+            if j == 0:
+                back_out[side] = part
+            else:
+                back_out[side] += part
+    for side in range(2):
+        side_copy(side, back_out, back_in, back_send, back_recv).start()
+    for side in range(2):
+        side_copy(side, back_out, back_in, back_send, back_recv).wait_recv()
+
+    own_back = one_hot((kmax, ROWS), lambda k, p: p == k + excess)
+    live = lax.broadcasted_iota(jnp.int32, (kmax, wide), 0) < here
+    for j in range(groups):
+        cols = slice(j * wide, (j + 1) * wide)
+        left_back = one_hot(
+            (kmax, ROWS), lambda k, r: (r == j * halo + halo + excess + k) & (k + excess < 0)
+        )
+        right_back = one_hot(
+            (kmax, ROWS),
+            lambda k, r: (r == j * halo + excess + k - BAL)
+            & (k + excess >= BAL) & (k + excess < BAL + halo),
+        )
+        got = (
+            place(own_back, branch[:, cols])
+            + place(left_back, back_in[0])
+            + place(right_back, back_in[1])
+        )
+        summed = g_ref[:, cols].astype(jnp.float32) + got
+        out_ref[:, cols] = jnp.where(live, summed, 0.0).astype(jnp.bfloat16)
+
+    for k in range(1, n_dp):
+        count_copy(k, me).wait_send()
+    for side in range(2):
+        side_copy(side, halo_out, halo_in, halo_send, halo_recv).wait_send()
+        side_copy(side, back_out, back_in, back_send, back_recv).wait_send()
+
+    @pl.loop(0, chunks)
+    def _(c):
+        for k in range(1, n_t):
+            in_copy(k, c, t).wait_send()
+            term_copy(k, c, t).wait_send()
+
+
+def fused(kept_input, kept_grad, up_weight_t, up_bias, down_weight, kept_count):
+    n_dp, n_t = lax.axis_size("dp"), lax.axis_size("tensor")
+    kmax, width = kept_input.shape
+    hidden = up_weight_t.shape[0]
+    chunks = width // COLS
+    wide = width // (ROWS // (BAL // 4))
+    tokens = n_t * ROWS
+    bf16, f32 = jnp.bfloat16, jnp.float32
+    vmem = pl.BlockSpec(memory_space=pltpu.VMEM)
+    smem = pl.BlockSpec(memory_space=pltpu.SMEM)
+    hbm = pl.BlockSpec(memory_space=pl.ANY)
+    dma = pltpu.SemaphoreType.DMA
+    return pl.pallas_call(
+        functools.partial(fused_kernel, n_dp, n_t),
+        out_shape=jax.ShapeDtypeStruct((kmax, width), bf16),
+        in_specs=[vmem, vmem, smem, vmem, hbm, hbm],
+        out_specs=vmem,
+        scratch_shapes=[
+            pltpu.VMEM((chunks, hidden, COLS), bf16),
+            pltpu.VMEM((chunks, hidden, COLS), bf16),
+            pltpu.VMEM((n_t, chunks, 2, ROWS, COLS), bf16),
+            pltpu.VMEM((chunks, n_t, ROWS, COLS), bf16),
+            pltpu.VMEM((n_t, chunks, ROWS, COLS), bf16),
+            pltpu.VMEM((ROWS, width), bf16),
+            pltpu.VMEM((tokens, hidden), f32),
+            pltpu.VMEM((tokens, hidden), f32),
+            pltpu.VMEM((tokens, hidden), bf16),
+            pltpu.VMEM((8, 128), jnp.int32),
+            pltpu.VMEM((n_dp, 8, 128), jnp.int32),
+            pltpu.VMEM((2, 2, ROWS, wide), bf16),
+            pltpu.VMEM((2, 2, ROWS, wide), bf16),
+            pltpu.VMEM((2, ROWS, wide), bf16),
+            pltpu.VMEM((2, ROWS, wide), bf16),
+            dma((2, chunks)),
+            dma((n_dp - 1,)),
+            dma((n_dp,)),
+            dma((2,)),
+            dma((2,)),
+            dma((2,)),
+            dma((2,)),
+            dma((n_t - 1, chunks)),
+            dma((n_t, chunks)),
+            dma((n_t - 1, chunks)),
+            dma((n_t, chunks)),
+        ],
+        compiler_params=pltpu.CompilerParams(
+            collective_id=0, has_side_effects=True, vmem_limit_bytes=VMEM_LIMIT
+        ),
+    )(kept_input, kept_grad, kept_count, up_bias.reshape(1, hidden), up_weight_t, down_weight)
+
+
+def fits(mesh, kept_input, up_weight_t):
+    hidden = up_weight_t.shape[0] // mesh.shape["tensor"]
+    width = up_weight_t.shape[1]
+    weights = 2 * hidden * width * 2
+    return (
+        hidden % ROWS == 0
+        and width % (COLS * 4) == 0
+        and BAL == ROWS
+        and mesh.shape["dp"] > 1
+        and mesh.shape["tensor"] > 1
+        and weights < VMEM_LIMIT * 3 // 4
+    )
+
+
 def solution(mesh):
-    placed = (
-        P(("dp", "tensor"), None),
-        P(("dp", "tensor"), None),
-        P("tensor", None),
-        P("tensor"),
-        P("tensor", None),
-        P(("dp", "tensor")),
-    )
-    return jax.shard_map(
-        body, mesh=mesh, in_specs=placed, out_specs=P(("dp", "tensor"), None), check_vma=False
-    )
+    rows = P(("dp", "tensor"), None)
+    placed = (rows, rows, P("tensor", None), P("tensor"), P("tensor", None), P(("dp", "tensor")))
+
+    def run(kept_input, kept_grad, up_weight_t, up_bias, down_weight, kept_count):
+        chosen = fused if fits(mesh, kept_input, up_weight_t) else body
+        return jax.shard_map(
+            chosen, mesh=mesh, in_specs=placed, out_specs=rows, check_vma=False
+        )(kept_input, kept_grad, up_weight_t, up_bias, down_weight, kept_count)
+
+    return run

time: 135 us -> 58.2 us (0.43)
  Pallas kernels: 0 us -> 54.4 us
  waiting for transfers between devices: 52.9 us -> 0 us
  matrix products: 31.7 us -> 0 us
  starting transfers between devices: 13.8 us -> 0 us
  between operations: 14.2 us -> 0.66 us
  blocking collectives: 7.3 us -> 0 us
  local copies, waits for them, and re-layouts: 8.2 us -> 2.91 us
  loops' own time: 5.22 us -> 0 us
  other arithmetic: 1.65 us -> 0 us
    pallas_call x0 -> x1, Pallas kernels: none -> 54.4 us  [fused(): pl.pallas_call(functools.partial(fused_kernel, n_dp, n_t), out_shape=jax....]
    dot_general x4 -> x0, matrix products: 31.7 us -> none  [the longest x1 17.2 us: ffn_rows(): jnp.dot(pre_grad, up_weight_t, preferred_element_type=jnp.float32)]
    all_gather x1 -> x0, waiting for transfers between devices: 28.6 us -> none  [ffn_rows(): piece_rows = lax.all_gather(stacked, 'tensor', axis=0, tiled=True)]
    reduce_scatter x1 -> x0, waiting for transfers between devices: 19.7 us -> none  [ffn_rows(): lax.psum_scatter(partials.astype(jnp.bfloat16), 'tensor', scatter_dimensi...]
    ppermute x4 -> x0, starting transfers between devices: 13.7 us -> none  [the longest x2 7.66 us: padded(): lax.ppermute(lax.slice_in_dim(block, block.shape[dim] - width, None, axis...]
    unnamed x1 -> x0, blocking collectives: 7.3 us -> none
    another operation x1 -> x0, loops' own time: 5.22 us -> none  [prefix(): return lax.fori_loop(0, length, lap, start)]
    dynamic_slice x8 -> x0, local copies, waits for them, and re-layouts: 5.2 us -> none  [lap(): new = combine(before, everything[k])]
  transfers between devices with their start and end apart: 6 -> 0, of which waited for: 4 -> 0; matrix products, arithmetic and copies ran while one was open for 1% -> 0% of each run, Pallas kernels for 0% -> 0%
where the time goes in v1:
time: 58.2 us; the launch traced here: 58 us
  Pallas kernels  54.4 us (93%)
  local copies, waits for them, and re-layouts  2.91 us (5%)
  between operations  0.66 us (1%)
    pallas_call x1, Pallas kernels, fused(): pl.pallas_call(functools.partial(fused_kernel, n_dp, n_t), out_shape=jax....  54.4 us
    unnamed x1, local copies, waits for them, and re-layouts  1.62 us
    reshape x1, local copies, waits for them, and re-layouts, fused(): up_bias.reshape(1, hidden)  1.3 us

profile of v1, /device:TPU:1, one launch (start us, length us, event | category | flops | bytes accessed | tf_op | source)
XLA Modules:
  0.0 58.0 jit_solution(3543264151478662484)
XLA Ops:
  0.7 1.3 %reshape.3.bias_ref = bf16[1,2064]{1,0:T(2,128)(2,1)} reshape(bf16[2064]{0:T(1024)(128)(2,1)} %param.9) | data formatting | bytes 8256 | tf_op jit(solution)/shard_map/reshape | solution.py:376
  1.9 54.4 %shard_map.64 = bf16[24,4096]{1,0:T(8,128)(2,1)} custom-call(bf16[24,4096]{1,0:T(8,128)(2,1)} %x_ref.1, bf16[24,4096]{1,0:T(8,128)(2,1)} %g_ref.1, s32[1]{0:T(128)S(6)} %copy.8.count_ref, bf16[1,2064]{1,0:T(2,128)(2,1)} %reshape.3.bias_ref, bf16[2064,4096]{1,0:T(8,128)(2,1)} %up_hbm.1, bf16[2064,4096]{1,0:T(8,128)(2,1)} %down_hbm.1), custom_call_target="tpu_custom_call" | custom-call | tf_op jit(solution)/shard_map/pallas_call | solution.py:340
  56.4 1.6 %copy.9 = bf16[24,4096]{1,0:T(8,128)(2,1)} copy(bf16[24,4096]{1,0:T(8,128)(2,1)} %shard_map.64) | data formatting | bytes 393216

commit v2 on v1

--- a/solution.py
+++ b/solution.py
@@ -122,7 +122,7 @@
 
 def fused_kernel(
     n_dp, n_t, x_ref, g_ref, count_ref, bias_ref, up_hbm, down_hbm, out_ref,
-    up, down, rows_in, terms, taken, branch, acc_x, acc_g, slopes,
+    up, down, rows_in, terms, taken, branch, acc, slopes, pre_grad,
     count_own, counts, halo_out, halo_in, back_out, back_in,
     w_sem, count_send, count_recv, halo_send, halo_recv, back_send, back_recv,
     in_send, in_recv, term_send, term_recv,
@@ -130,25 +130,24 @@
     me = lax.axis_index("dp")
     t = lax.axis_index("tensor")
     kmax, width = x_ref.shape
-    chunks = width // COLS
     halo = BAL // 4
     groups = ROWS // halo
     wide = width // groups
+    narrow = wide // groups
     per_group = wide // COLS
+    chunks = width // COLS
+    steps = 2 * groups
     left = lax.rem(me + n_dp - 1, n_dp)
     right = lax.rem(me + 1, n_dp)
 
-    def weight_copies(c):
-        cols = pl.ds(pl.multiple_of(c * COLS, COLS), COLS)
-        return (
-            pltpu.make_async_copy(up_hbm.at[:, cols], up.at[c], w_sem.at[0, c]),
-            pltpu.make_async_copy(down_hbm.at[:, cols], down.at[c], w_sem.at[1, c]),
-        )
-
-    @pl.loop(0, chunks)
-    def _(c):
-        for copy in weight_copies(c):
-            copy.start()
+    def weight_copy(i, j):
+        source, target = ((up_hbm, up), (down_hbm, down))[i]
+        cols = pl.ds(pl.multiple_of(j * wide, wide), wide)
+        return pltpu.make_async_copy(source.at[:, cols], target.at[j], w_sem.at[i, j])
+
+    for i in range(2):
+        for j in range(groups):
+            weight_copy(i, j).start()
 
     barrier = pltpu.get_barrier_semaphore()
     for k in range(1, n_dp):
@@ -162,19 +161,16 @@
 
     here = count_ref[0]
     count_own[...] = jnp.full(count_own.shape, here, jnp.int32)
-    for j in range(groups):
-        cols = slice(j * wide, (j + 1) * wide)
-        head = one_hot((ROWS, kmax), lambda r, k: (r // halo == j) & (k == r % halo))
-        tail = one_hot(
-            (ROWS, kmax), lambda r, k: (r // halo == j) & (k == here - halo + r % halo)
-        )
+    for side in range(2):
+        first = (here - halo) if side else 0
         for i, ref in enumerate((x_ref, g_ref)):
-            for side, matrix in enumerate((head, tail)):
-                part = place(matrix, ref[:, cols]).astype(jnp.bfloat16)
-                if j == 0:
-                    halo_out[side, i] = part
-                else:
-                    halo_out[side, i] += part
+            packed = jnp.zeros((ROWS, wide), jnp.float32)
+            for j in range(groups):
+                picked = one_hot(
+                    (ROWS, kmax), lambda r, k: (r // halo == j) & (k == first + r % halo)
+                )
+                packed = packed + place(picked, ref[:, j * wide : (j + 1) * wide])
+            halo_out[side, i] = packed.astype(jnp.bfloat16)
     pl.semaphore_wait(barrier, n_dp - 1 + n_t - 1)
 
     def count_copy(k, source):
@@ -184,17 +180,25 @@
             device_id={"dp": lax.rem(me + k, n_dp)}, device_id_type=MESH,
         )
 
-    def side_copy(side, source, target, send, recv):
+    def halo_copy(side, i):
         return pltpu.make_async_remote_copy(
-            src_ref=source.at[side], dst_ref=target.at[1 - side],
-            send_sem=send.at[side], recv_sem=recv.at[1 - side],
+            src_ref=halo_out.at[side, i], dst_ref=halo_in.at[1 - side, i],
+            send_sem=halo_send.at[side, i], recv_sem=halo_recv.at[1 - side, i],
             device_id={"dp": right if side else left}, device_id_type=MESH,
         )
 
-    for side in range(2):
-        side_copy(side, halo_out, halo_in, halo_send, halo_recv).start()
+    def back_copy(side, j):
+        return pltpu.make_async_remote_copy(
+            src_ref=back_out.at[side, j], dst_ref=back_in.at[1 - side, j],
+            send_sem=back_send.at[side, j], recv_sem=back_recv.at[1 - side, j],
+            device_id={"dp": right if side else left}, device_id_type=MESH,
+        )
+
     for k in range(1, n_dp):
         count_copy(k, me).start()
+    for i in range(2):
+        for side in range(2):
+            halo_copy(side, i).start()
     for k in range(1, n_dp):
         count_copy(k, lax.rem(me + n_dp - k, n_dp)).wait_recv()
     before = jnp.zeros(count_own.shape, jnp.int32)
@@ -203,54 +207,71 @@
     excess = (before - me * BAL)[0:1, 0:1]
     following = excess + here - BAL
 
-    def in_copy(k, c, source):
+    def in_copy(up_line, source, step):
         return pltpu.make_async_remote_copy(
-            src_ref=rows_in.at[source, c], dst_ref=rows_in.at[source, c],
-            send_sem=in_send.at[k - 1, c], recv_sem=in_recv.at[source, c],
-            device_id={"tensor": lax.rem(t + k, n_t)}, device_id_type=MESH,
-        )
-
-    own_at = one_hot(
-        (ROWS, kmax), lambda p, k: (k == p - excess) & (k < here)
-    )
-    for side in range(2):
-        side_copy(side, halo_out, halo_in, halo_send, halo_recv).wait_recv()
+            src_ref=rows_in.at[source, step], dst_ref=rows_in.at[source, step],
+            send_sem=in_send.at[up_line, source, step], recv_sem=in_recv.at[source, step],
+            device_id={"tensor": t + 1 if up_line else t - 1}, device_id_type=MESH,
+        )
+
+    def pass_on(source, step, up_line, down_line):
+        if up_line:
+            @pl.when(t < n_t - 1)
+            def _():
+                in_copy(1, source, step).start()
+        if down_line:
+            @pl.when(t > 0)
+            def _():
+                in_copy(0, source, step).start()
+
+    own_at = one_hot((ROWS, kmax), lambda p, k: (k == p - excess) & (k < here))
+    from_left, from_right = [], []
     for j in range(groups):
-        cols = slice(j * wide, (j + 1) * wide)
-        from_left = one_hot(
+        from_left.append(one_hot(
             (ROWS, ROWS), lambda p, r: (r == j * halo + halo - excess + p) & (p < excess)
-        )
-        from_right = one_hot(
+        ))
+        from_right.append(one_hot(
             (ROWS, ROWS),
             lambda p, r: (r == j * halo + p - BAL - following) & (p >= BAL + following),
-        )
-        for i, ref in enumerate((x_ref, g_ref)):
-            window = (
-                place(own_at, ref[:, cols])
-                + place(from_left, halo_in[0, i])
-                + place(from_right, halo_in[1, i])
+        ))
+    for i, ref in enumerate((x_ref, g_ref)):
+        for side in range(2):
+            halo_copy(side, i).wait_recv()
+        for j in range(groups):
+            rows_in[t, i * groups + j] = (
+                place(own_at, ref[:, j * wide : (j + 1) * wide])
+                + place(from_left[j], halo_in[0, i])
+                + place(from_right[j], halo_in[1, i])
             ).astype(jnp.bfloat16)
-            for s in range(per_group):
-                rows_in[t, j * per_group + s, i] = window[:, s * COLS : (s + 1) * COLS]
-        for s in range(per_group):
-            for k in range(1, n_t):
-                in_copy(k, j * per_group + s, t).start()
-
-    acc_x[...] = jnp.broadcast_to(bias_ref[...].astype(jnp.float32), acc_x.shape)
-    acc_g[...] = jnp.zeros_like(acc_g)
-
-    @pl.loop(0, chunks)
-    def _(c):
-        for copy in weight_copies(c):
-            copy.wait()
-        for k in range(1, n_t):
-            in_copy(k, c, lax.rem(t + n_t - k, n_t)).wait_recv()
-        x = rows_in[:, c, 0].reshape(n_t * ROWS, COLS)
-        g = rows_in[:, c, 1].reshape(n_t * ROWS, COLS)
-        acc_x[...] += lax.dot_general(x, up[c], NT, preferred_element_type=jnp.float32)
-        acc_g[...] += lax.dot_general(g, down[c], NT, preferred_element_type=jnp.float32)
-
-    slopes[...] = (gelu_slope(acc_x[...]) * acc_g[...]).astype(jnp.bfloat16)
+            pass_on(t, i * groups + j, True, True)
+
+    def multiply(i, weights, first):
+        acc[...] = first
+
+        @pl.loop(0, groups)
+        def _(j):
+            step = i * groups + j
+            for d in range(1, n_t):
+                @pl.when(t - d >= 0)
+                def _():
+                    in_copy(1, t - d, step).wait_recv()
+                    pass_on(t - d, step, True, False)
+
+                @pl.when(t + d < n_t)
+                def _():
+                    in_copy(0, t + d, step).wait_recv()
+                    pass_on(t + d, step, False, True)
+            weight_copy(i, j).wait()
+            block = rows_in[:, step].reshape(n_t * ROWS, wide)
+            acc[...] += lax.dot_general(
+                block, weights[j], NT, preferred_element_type=jnp.float32
+            )
+
+    bias = bias_ref[...].astype(jnp.float32).reshape(1, acc.shape[1])
+    multiply(0, up, jnp.broadcast_to(bias, acc.shape))
+    slopes[...] = gelu_slope(acc[...])
+    multiply(1, down, jnp.zeros(acc.shape, jnp.float32))
+    pre_grad[...] = (slopes[...] * acc[...]).astype(jnp.bfloat16)
 
     def term_copy(k, c, source):
         dest = lax.rem(t + k, n_t)
@@ -260,68 +281,87 @@
             device_id={"tensor": dest}, device_id_type=MESH,
         )
 
-    @pl.loop(0, chunks)
-    def _(c):
-        term = jnp.dot(slopes[...], up[c], preferred_element_type=jnp.float32)
-        terms[c] = term.astype(jnp.bfloat16).reshape(n_t, ROWS, COLS)
-        for k in range(1, n_t):
-            term_copy(k, c, t).start()
-
-    for c in range(chunks):
-        total = terms[c, t].astype(jnp.float32)
-        for k in range(1, n_t):
-            source = lax.rem(t + n_t - k, n_t)
-            term_copy(k, c, source).wait_recv()
-            total = total + taken[source, c].astype(jnp.float32)
-        branch[:, c * COLS : (c + 1) * COLS] = total.astype(jnp.bfloat16)
+    @pl.loop(0, groups)
+    def _(j):
+        for s in range(per_group):
+            c = j * per_group + s
+            term = jnp.dot(
+                pre_grad[...], up[j, :, s * COLS : (s + 1) * COLS],
+                preferred_element_type=jnp.float32,
+            )
+            terms[c] = term.astype(jnp.bfloat16).reshape(n_t, ROWS, COLS)
+            for k in range(1, n_t):
+                term_copy(k, c, t).start()
 
     for j in range(groups):
-        cols = slice(j * wide, (j + 1) * wide)
-        head = one_hot((ROWS, ROWS), lambda r, p: (r // halo == j) & (p == r % halo))
-        tail = one_hot(
-            (ROWS, ROWS), lambda r, p: (r // halo == j) & (p == BAL - halo + r % halo)
-        )
-        for side, matrix in enumerate((head, tail)):
-            part = place(matrix, branch[:, cols]).astype(jnp.bfloat16)
-            if j == 0:
-                back_out[side] = part
-            else:
-                back_out[side] += part
-    for side in range(2):
-        side_copy(side, back_out, back_in, back_send, back_recv).start()
-    for side in range(2):
-        side_copy(side, back_out, back_in, back_send, back_recv).wait_recv()
+        for s in range(per_group):
+            c = j * per_group + s
+            total = terms[c, t].astype(jnp.float32)
+            for k in range(1, n_t):
+                source = lax.rem(t + n_t - k, n_t)
+                term_copy(k, c, source).wait_recv()
+                total = total + taken[source, c].astype(jnp.float32)
+            branch[:, c * COLS : (c + 1) * COLS] = total.astype(jnp.bfloat16)
+        for side in range(2):
+            first = (BAL - halo) if side else 0
+            packed = jnp.zeros((ROWS, narrow), jnp.float32)
+            for q in range(groups):
+                picked = one_hot(
+                    (ROWS, ROWS), lambda r, p: (r // halo == q) & (p == first + r % halo)
+                )
+                start = j * wide + q * narrow
+                packed = packed + place(picked, branch[:, start : start + narrow])
+            back_out[side, j] = packed.astype(jnp.bfloat16)
+            back_copy(side, j).start()
 
     own_back = one_hot((kmax, ROWS), lambda k, p: p == k + excess)
-    live = lax.broadcasted_iota(jnp.int32, (kmax, wide), 0) < here
+    live = lax.broadcasted_iota(jnp.int32, (kmax, narrow), 0) < here
+    left_back, right_back = [], []
+    for q in range(groups):
+        left_back.append(one_hot(
+            (kmax, ROWS), lambda k, r: (r == q * halo + halo + excess + k) & (k + excess < 0)
+        ))
+        right_back.append(one_hot(
+            (kmax, ROWS),
+            lambda k, r: (r == q * halo + excess + k - BAL)
+            & (k + excess >= BAL) & (k + excess < BAL + halo),
+        ))
     for j in range(groups):
-        cols = slice(j * wide, (j + 1) * wide)
-        left_back = one_hot(
-            (kmax, ROWS), lambda k, r: (r == j * halo + halo + excess + k) & (k + excess < 0)
-        )
-        right_back = one_hot(
-            (kmax, ROWS),
-            lambda k, r: (r == j * halo + excess + k - BAL)
-            & (k + excess >= BAL) & (k + excess < BAL + halo),
-        )
-        got = (
-            place(own_back, branch[:, cols])
-            + place(left_back, back_in[0])
-            + place(right_back, back_in[1])
-        )
-        summed = g_ref[:, cols].astype(jnp.float32) + got
-        out_ref[:, cols] = jnp.where(live, summed, 0.0).astype(jnp.bfloat16)
+        for side in range(2):
+            back_copy(side, j).wait_recv()
+        for q in range(groups):
+            start = j * wide + q * narrow
+            cols = slice(start, start + narrow)
+            got = (
+                place(own_back, branch[:, cols])
+                + place(left_back[q], back_in[0, j])
+                + place(right_back[q], back_in[1, j])
+            )
+            summed = g_ref[:, cols].astype(jnp.float32) + got
+            out_ref[:, cols] = jnp.where(live, summed, 0.0).astype(jnp.bfloat16)
 
     for k in range(1, n_dp):
         count_copy(k, me).wait_send()
     for side in range(2):
-        side_copy(side, halo_out, halo_in, halo_send, halo_recv).wait_send()
-        side_copy(side, back_out, back_in, back_send, back_recv).wait_send()
+        for i in range(2):
+            halo_copy(side, i).wait_send()
+        for j in range(groups):
+            back_copy(side, j).wait_send()
+
+    @pl.loop(0, steps)
+    def _(step):
+        for j in range(n_t):
+            @pl.when((j <= t) & (t < n_t - 1))
+            def _():
+                in_copy(1, j, step).wait_send()
+
+            @pl.when((j >= t) & (t > 0))
+            def _():
+                in_copy(0, j, step).wait_send()
 
     @pl.loop(0, chunks)
     def _(c):
         for k in range(1, n_t):
-            in_copy(k, c, t).wait_send()
             term_copy(k, c, t).wait_send()
 
 
@@ -330,7 +370,10 @@
     kmax, width = kept_input.shape
     hidden = up_weight_t.shape[0]
     chunks = width // COLS
-    wide = width // (ROWS // (BAL // 4))
+    groups = ROWS // (BAL // 4)
+    wide = width // groups
+    narrow = wide // groups
+    steps = 2 * groups
     tokens = n_t * ROWS
     bf16, f32 = jnp.bfloat16, jnp.float32
     vmem = pl.BlockSpec(memory_space=pltpu.VMEM)
@@ -343,9 +386,9 @@
         in_specs=[vmem, vmem, smem, vmem, hbm, hbm],
         out_specs=vmem,
         scratch_shapes=[
-            pltpu.VMEM((chunks, hidden, COLS), bf16),
-            pltpu.VMEM((chunks, hidden, COLS), bf16),
-            pltpu.VMEM((n_t, chunks, 2, ROWS, COLS), bf16),
+            pltpu.VMEM((groups, hidden, wide), bf16),
+            pltpu.VMEM((groups, hidden, wide), bf16),
+            pltpu.VMEM((n_t, steps, ROWS, wide), bf16),
             pltpu.VMEM((chunks, n_t, ROWS, COLS), bf16),
             pltpu.VMEM((n_t, chunks, ROWS, COLS), bf16),
             pltpu.VMEM((ROWS, width), bf16),
@@ -356,24 +399,24 @@
             pltpu.VMEM((n_dp, 8, 128), jnp.int32),
             pltpu.VMEM((2, 2, ROWS, wide), bf16),
             pltpu.VMEM((2, 2, ROWS, wide), bf16),
-            pltpu.VMEM((2, ROWS, wide), bf16),
-            pltpu.VMEM((2, ROWS, wide), bf16),
-            dma((2, chunks)),
+            pltpu.VMEM((2, groups, ROWS, narrow), bf16),
+            pltpu.VMEM((2, groups, ROWS, narrow), bf16),
+            dma((2, groups)),
             dma((n_dp - 1,)),
             dma((n_dp,)),
-            dma((2,)),
-            dma((2,)),
-            dma((2,)),
-            dma((2,)),
-            dma((n_t - 1, chunks)),
-            dma((n_t, chunks)),
+            dma((2, 2)),
+            dma((2, 2)),
+            dma((2, groups)),
+            dma((2, groups)),
+            dma((2, n_t, steps)),
+            dma((n_t, steps)),
             dma((n_t - 1, chunks)),
             dma((n_t, chunks)),
         ],
         compiler_params=pltpu.CompilerParams(
             collective_id=0, has_side_effects=True, vmem_limit_bytes=VMEM_LIMIT
         ),
-    )(kept_input, kept_grad, kept_count, up_bias.reshape(1, hidden), up_weight_t, down_weight)
+    )(kept_input, kept_grad, kept_count, up_bias, up_weight_t, down_weight)
 
 
 def fits(mesh, kept_input, up_weight_t):

time: 58.2 us -> 68.8 us (1.18)
  Pallas kernels: 54.4 us -> 66.4 us
  local copies, waits for them, and re-layouts: 2.91 us -> 1.62 us
    pallas_call x1, Pallas kernels: 54.4 us -> 66.4 us  [fused(): pl.pallas_call(functools.partial(fused_kernel, n_dp, n_t), out_shape=jax....]
    reshape x1 -> x0, local copies, waits for them, and re-layouts: 1.3 us -> none  [fused(): up_bias.reshape(1, hidden)]
where the time goes in v2:
time: 68.8 us; the launch traced here: 68.7 us
  Pallas kernels  66.4 us (97%)
  local copies, waits for them, and re-layouts  1.62 us (2%)
    pallas_call x1, Pallas kernels, fused(): pl.pallas_call(functools.partial(fused_kernel, n_dp, n_t), out_shape=jax....  66.4 us
    unnamed x1, local copies, waits for them, and re-layouts  1.62 us

profile of v2, /device:TPU:1, one launch (start us, length us, event | category | flops | bytes accessed | tf_op | source)
XLA Modules:
  0.0 68.7 jit_solution(7365797880145737255)
XLA Ops:
  0.7 66.4 %shard_map.64 = bf16[24,4096]{1,0:T(8,128)(2,1)} custom-call(bf16[24,4096]{1,0:T(8,128)(2,1)} %x_ref.1, bf16[24,4096]{1,0:T(8,128)(2,1)} %g_ref.1, s32[1]{0:T(128)S(6)} %copy.8.count_ref, bf16[2064]{0:T(1024)(128)(2,1)} %bias_ref.1, bf16[2064,4096]{1,0:T(8,128)(2,1)} %up_hbm.1, bf16[2064,4096]{1,0:T(8,128)(2,1)} %down_hbm.1), custom_call_target="tpu_custom_call" | custom-call | tf_op jit(solution)/shard_map/pallas_call | solution.py:383
  67.1 1.6 %copy.9 = bf16[24,4096]{1,0:T(8,128)(2,1)} copy(bf16[24,4096]{1,0:T(8,128)(2,1)} %shard_map.64) | data formatting | bytes 393216

commit v3 on v2

--- a/solution.py
+++ b/solution.py
@@ -207,22 +207,12 @@
     excess = (before - me * BAL)[0:1, 0:1]
     following = excess + here - BAL
 
-    def in_copy(up_line, source, step):
+    def in_copy(k, source, step):
         return pltpu.make_async_remote_copy(
             src_ref=rows_in.at[source, step], dst_ref=rows_in.at[source, step],
-            send_sem=in_send.at[up_line, source, step], recv_sem=in_recv.at[source, step],
-            device_id={"tensor": t + 1 if up_line else t - 1}, device_id_type=MESH,
-        )
-
-    def pass_on(source, step, up_line, down_line):
-        if up_line:
-            @pl.when(t < n_t - 1)
-            def _():
-                in_copy(1, source, step).start()
-        if down_line:
-            @pl.when(t > 0)
-            def _():
-                in_copy(0, source, step).start()
+            send_sem=in_send.at[k - 1, step], recv_sem=in_recv.at[source, step],
+            device_id={"tensor": lax.rem(t + k, n_t)}, device_id_type=MESH,
+        )
 
     own_at = one_hot((ROWS, kmax), lambda p, k: (k == p - excess) & (k < here))
     from_left, from_right = [], []
@@ -243,7 +233,8 @@
                 + place(from_left[j], halo_in[0, i])
                 + place(from_right[j], halo_in[1, i])
             ).astype(jnp.bfloat16)
-            pass_on(t, i * groups + j, True, True)
+            for k in range(1, n_t):
+                in_copy(k, t, i * groups + j).start()
 
     def multiply(i, weights, first):
         acc[...] = first
@@ -251,16 +242,8 @@
         @pl.loop(0, groups)
         def _(j):
             step = i * groups + j
-            for d in range(1, n_t):
-                @pl.when(t - d >= 0)
-                def _():
-                    in_copy(1, t - d, step).wait_recv()
-                    pass_on(t - d, step, True, False)
-
-                @pl.when(t + d < n_t)
-                def _():
-                    in_copy(0, t + d, step).wait_recv()
-                    pass_on(t + d, step, False, True)
+            for k in range(1, n_t):
+                in_copy(k, lax.rem(t + n_t - k, n_t), step).wait_recv()
             weight_copy(i, j).wait()
             block = rows_in[:, step].reshape(n_t * ROWS, wide)
             acc[...] += lax.dot_general(
@@ -350,14 +333,8 @@
 
     @pl.loop(0, steps)
     def _(step):
-        for j in range(n_t):
-            @pl.when((j <= t) & (t < n_t - 1))
-            def _():
-                in_copy(1, j, step).wait_send()
-
-            @pl.when((j >= t) & (t > 0))
-            def _():
-                in_copy(0, j, step).wait_send()
+        for k in range(1, n_t):
+            in_copy(k, t, step).wait_send()
 
     @pl.loop(0, chunks)
     def _(c):
@@ -408,7 +385,7 @@
             dma((2, 2)),
             dma((2, groups)),
             dma((2, groups)),
-            dma((2, n_t, steps)),
+            dma((n_t - 1, steps)),
             dma((n_t, steps)),
             dma((n_t - 1, chunks)),
             dma((n_t, chunks)),

time: 68.8 us -> 55.6 us (0.81)
  Pallas kernels: 66.4 us -> 53.1 us
    pallas_call x1, Pallas kernels: 66.4 us -> 53.1 us  [fused(): pl.pallas_call(functools.partial(fused_kernel, n_dp, n_t), out_shape=jax....]
where the time goes in v3:
time: 55.6 us; the launch traced here: 55.4 us
  Pallas kernels  53.1 us (96%)
  local copies, waits for them, and re-layouts  1.62 us (3%)
  between operations  0.66 us (1%)
    pallas_call x1, Pallas kernels, fused(): pl.pallas_call(functools.partial(fused_kernel, n_dp, n_t), out_shape=jax....  53.1 us
    unnamed x1, local copies, waits for them, and re-layouts  1.62 us

profile of v3, /device:TPU:1, one launch (start us, length us, event | category | flops | bytes accessed | tf_op | source)
XLA Modules:
  0.0 55.4 jit_solution(14549047479104793076)
XLA Ops:
  0.7 53.1 %shard_map.64 = bf16[24,4096]{1,0:T(8,128)(2,1)} custom-call(bf16[24,4096]{1,0:T(8,128)(2,1)} %x_ref.1, bf16[24,4096]{1,0:T(8,128)(2,1)} %g_ref.1, s32[1]{0:T(128)S(6)} %copy.8.count_ref, bf16[2064]{0:T(1024)(128)(2,1)} %bias_ref.1, bf16[2064,4096]{1,0:T(8,128)(2,1)} %up_hbm.1, bf16[2064,4096]{1,0:T(8,128)(2,1)} %down_hbm.1), custom_call_target="tpu_custom_call" | custom-call | tf_op jit(solution)/shard_map/pallas_call | solution.py:360
  53.8 1.6 %copy.9 = bf16[24,4096]{1,0:T(8,128)(2,1)} copy(bf16[24,4096]{1,0:T(8,128)(2,1)} %shard_map.64) | data formatting | bytes 393216

commit v4 on v3

--- a/solution.py
+++ b/solution.py
@@ -236,8 +236,8 @@
             for k in range(1, n_t):
                 in_copy(k, t, i * groups + j).start()
 
-    def multiply(i, weights, first):
-        acc[...] = first
+    def multiply(i, weights):
+        acc[...] = jnp.zeros_like(acc)
 
         @pl.loop(0, groups)
         def _(j):
@@ -247,14 +247,14 @@
             weight_copy(i, j).wait()
             block = rows_in[:, step].reshape(n_t * ROWS, wide)
             acc[...] += lax.dot_general(
-                block, weights[j], NT, preferred_element_type=jnp.float32
+                weights[j], block, NT, preferred_element_type=jnp.float32
             )
 
-    bias = bias_ref[...].astype(jnp.float32).reshape(1, acc.shape[1])
-    multiply(0, up, jnp.broadcast_to(bias, acc.shape))
-    slopes[...] = gelu_slope(acc[...])
-    multiply(1, down, jnp.zeros(acc.shape, jnp.float32))
-    pre_grad[...] = (slopes[...] * acc[...]).astype(jnp.bfloat16)
+    bias = bias_ref[...].astype(jnp.float32).reshape(1, slopes.shape[1])
+    multiply(0, up)
+    slopes[...] = gelu_slope(acc[...].T + bias)
+    multiply(1, down)
+    pre_grad[...] = (slopes[...] * acc[...].T).astype(jnp.bfloat16)
 
     def term_copy(k, c, source):
         dest = lax.rem(t + k, n_t)
@@ -369,7 +369,7 @@
             pltpu.VMEM((chunks, n_t, ROWS, COLS), bf16),
             pltpu.VMEM((n_t, chunks, ROWS, COLS), bf16),
             pltpu.VMEM((ROWS, width), bf16),
-            pltpu.VMEM((tokens, hidden), f32),
+            pltpu.VMEM((hidden, tokens), f32),
             pltpu.VMEM((tokens, hidden), f32),
             pltpu.VMEM((tokens, hidden), bf16),
             pltpu.VMEM((8, 128), jnp.int32),

time: 55.6 us -> 55.7 us (level)
  no operation moved by 1% of the time
where the time goes in v4:
time: 55.7 us; the launch traced here: 55.5 us
  Pallas kernels  53.2 us (96%)
  local copies, waits for them, and re-layouts  1.62 us (3%)
  between operations  0.66 us (1%)
    pallas_call x1, Pallas kernels, fused(): pl.pallas_call(functools.partial(fused_kernel, n_dp, n_t), out_shape=jax....  53.2 us
    unnamed x1, local copies, waits for them, and re-layouts  1.62 us

profile of v4, /device:TPU:1, one launch (start us, length us, event | category | flops | bytes accessed | tf_op | source)
XLA Modules:
  0.0 55.5 jit_solution(17484546607630648889)
XLA Ops:
  0.7 53.2 %shard_map.64 = bf16[24,4096]{1,0:T(8,128)(2,1)} custom-call(bf16[24,4096]{1,0:T(8,128)(2,1)} %x_ref.1, bf16[24,4096]{1,0:T(8,128)(2,1)} %g_ref.1, s32[1]{0:T(128)S(6)} %copy.8.count_ref, bf16[2064]{0:T(1024)(128)(2,1)} %bias_ref.1, bf16[2064,4096]{1,0:T(8,128)(2,1)} %up_hbm.1, bf16[2064,4096]{1,0:T(8,128)(2,1)} %down_hbm.1), custom_call_target="tpu_custom_call" | custom-call | tf_op jit(solution)/shard_map/pallas_call | solution.py:360
  53.9 1.6 %copy.9 = bf16[24,4096]{1,0:T(8,128)(2,1)} copy(bf16[24,4096]{1,0:T(8,128)(2,1)} %shard_map.64) | data formatting | bytes 393216

commit v5 on v3

--- a/solution.py
+++ b/solution.py
@@ -105,6 +105,7 @@
 
 ROWS = 16
 COLS = 512
+LEAD = 3
 VMEM_LIMIT = 58 * 1024 * 1024
 MESH = pl.DeviceIdType.MESH
 NT = (((1,), (1,)), ((), ()))
@@ -125,7 +126,7 @@
     up, down, rows_in, terms, taken, branch, acc, slopes, pre_grad,
     count_own, counts, halo_out, halo_in, back_out, back_in,
     w_sem, count_send, count_recv, halo_send, halo_recv, back_send, back_recv,
-    in_send, in_recv, term_send, term_recv,
+    in_send, in_recv, relay_send, term_send, term_recv,
 ):
     me = lax.axis_index("dp")
     t = lax.axis_index("tensor")
@@ -213,6 +214,29 @@
             send_sem=in_send.at[k - 1, step], recv_sem=in_recv.at[source, step],
             device_id={"tensor": lax.rem(t + k, n_t)}, device_id_type=MESH,
         )
+
+    def relay_copy(source, step):
+        return pltpu.make_async_remote_copy(
+            src_ref=rows_in.at[source, step], dst_ref=rows_in.at[source, step],
+            send_sem=relay_send.at[0 if source else 1, step],
+            recv_sem=in_recv.at[source, step],
+            device_id={"tensor": n_t - 1 - source}, device_id_type=MESH,
+        )
+
+    relays = (0, n_t - 1) if n_t > 2 else ()
+
+    def relay_at(source):
+        return t == (1 if source else n_t - 2)
+
+    def sends(k):
+        dest = lax.rem(t + k, n_t)
+        return jnp.abs(dest - t) < n_t - (1 if relays else 0)
+
+    def start_own(step):
+        for k in range(1, n_t):
+            @pl.when(sends(k))
+            def _():
+                in_copy(k, t, step).start()
 
     own_at = one_hot((ROWS, kmax), lambda p, k: (k == p - excess) & (k < here))
     from_left, from_right = [], []
@@ -233,8 +257,8 @@
                 + place(from_left[j], halo_in[0, i])
                 + place(from_right[j], halo_in[1, i])
             ).astype(jnp.bfloat16)
-            for k in range(1, n_t):
-                in_copy(k, t, i * groups + j).start()
+            if i * groups + j < LEAD:
+                start_own(i * groups + j)
 
     def multiply(i, weights, first):
         acc[...] = first
@@ -242,8 +266,26 @@
         @pl.loop(0, groups)
         def _(j):
             step = i * groups + j
+            for source in relays:
+                @pl.when(relay_at(source))
+                def _():
+                    in_copy(1, source, step).wait_recv()
+                    relay_copy(source, step).start()
+
+            @pl.when(step + LEAD < steps)
+            def _():
+                start_own(step + LEAD)
+
             for k in range(1, n_t):
-                in_copy(k, lax.rem(t + n_t - k, n_t), step).wait_recv()
+                source = lax.rem(t + n_t - k, n_t)
+                waiting = k > 0
+                for end in relays:
+                    waiting = waiting & ((source != end) | jnp.logical_not(relay_at(end)))
+
+                @pl.when(waiting)
+                def _():
+                    in_copy(1, source, step).wait_recv()
+
             weight_copy(i, j).wait()
             block = rows_in[:, step].reshape(n_t * ROWS, wide)
             acc[...] += lax.dot_general(
@@ -334,7 +376,14 @@
     @pl.loop(0, steps)
     def _(step):
         for k in range(1, n_t):
-            in_copy(k, t, step).wait_send()
+            @pl.when(sends(k))
+            def _():
+                in_copy(k, t, step).wait_send()
+
+        for source in relays:
+            @pl.when(relay_at(source))
+            def _():
+                relay_copy(source, step).wait_send()
 
     @pl.loop(0, chunks)
     def _(c):
@@ -387,6 +436,7 @@
             dma((2, groups)),
             dma((n_t - 1, steps)),
             dma((n_t, steps)),
+            dma((2, steps)),
             dma((n_t - 1, chunks)),
             dma((n_t, chunks)),
         ],

time: 55.6 us -> 50.5 us (0.908)
  Pallas kernels: 53.1 us -> 48.1 us
    pallas_call x1, Pallas kernels: 53.1 us -> 48.1 us  [fused(): pl.pallas_call(functools.partial(fused_kernel, n_dp, n_t), out_shape=jax....]
where the time goes in v5:
time: 50.5 us; the launch traced here: 50.4 us
  Pallas kernels  48.1 us (95%)
  local copies, waits for them, and re-layouts  1.62 us (3%)
  between operations  0.66 us (1%)
    pallas_call x1, Pallas kernels, fused(): pl.pallas_call(functools.partial(fused_kernel, n_dp, n_t), out_shape=jax....  48.1 us
    unnamed x1, local copies, waits for them, and re-layouts  1.62 us

profile of v5, /device:TPU:1, one launch (start us, length us, event | category | flops | bytes accessed | tf_op | source)
XLA Modules:
  0.0 50.4 jit_solution(13896942057983797214)
XLA Ops:
  0.7 48.1 %shard_map.64 = bf16[24,4096]{1,0:T(8,128)(2,1)} custom-call(bf16[24,4096]{1,0:T(8,128)(2,1)} %x_ref.1, bf16[24,4096]{1,0:T(8,128)(2,1)} %g_ref.1, s32[1]{0:T(128)S(6)} %copy.8.count_ref, bf16[2064]{0:T(1024)(128)(2,1)} %bias_ref.1, bf16[2064,4096]{1,0:T(8,128)(2,1)} %up_hbm.1, bf16[2064,4096]{1,0:T(8,128)(2,1)} %down_hbm.1), custom_call_target="tpu_custom_call" | custom-call | tf_op jit(solution)/shard_map/pallas_call | solution.py:409
  48.8 1.6 %copy.9 = bf16[24,4096]{1,0:T(8,128)(2,1)} copy(bf16[24,4096]{1,0:T(8,128)(2,1)} %shard_map.64) | data formatting | bytes 393216

commit v6 on v5

--- a/solution.py
+++ b/solution.py
@@ -123,10 +123,10 @@
 
 def fused_kernel(
     n_dp, n_t, x_ref, g_ref, count_ref, bias_ref, up_hbm, down_hbm, out_ref,
-    up, down, rows_in, terms, taken, branch, acc, slopes, pre_grad,
+    up, down, rows_in, terms, taken, passing, branch, acc, slopes, pre_grad,
     count_own, counts, halo_out, halo_in, back_out, back_in,
     w_sem, count_send, count_recv, halo_send, halo_recv, back_send, back_recv,
-    in_send, in_recv, relay_send, term_send, term_recv,
+    in_send, in_recv, relay_send, term_send, term_recv, pass_recv,
 ):
     me = lax.axis_index("dp")
     t = lax.axis_index("tensor")
@@ -306,6 +306,43 @@
             device_id={"tensor": dest}, device_id_type=MESH,
         )
 
+    def far_copy(k, end, c):
+        return pltpu.make_async_remote_copy(
+            src_ref=terms.at[c, end], dst_ref=passing.at[0 if end else 1, c],
+            send_sem=term_send.at[k - 1, c], recv_sem=pass_recv.at[0 if end else 1, c],
+            device_id={"tensor": 1 if end else n_t - 2}, device_id_type=MESH,
+        )
+
+    def adds_for(end):
+        return t == (1 if end else n_t - 2)
+
+    def start_terms(c):
+        for end in relays:
+            @pl.when(t == n_t - 1 - end)
+            def _():
+                far_copy(n_t - 1 if end else 1, end, c).start()
+        for k in range(1, n_t):
+            dest = lax.rem(t + k, n_t)
+            direct = sends(k)
+            for end in relays:
+                direct = direct & ((dest != end) | jnp.logical_not(adds_for(end)))
+
+            @pl.when(direct)
+            def _():
+                term_copy(k, c, t).start()
+
+    def start_sums(c):
+        for end in relays:
+            @pl.when(adds_for(end))
+            def _():
+                k = n_t - 2 if end else 2
+                far_copy(1, end, c).wait_recv()
+                both = terms[c, end].astype(jnp.float32) + passing[
+                    0 if end else 1, c
+                ].astype(jnp.float32)
+                terms[c, end] = both.astype(jnp.bfloat16)
+                term_copy(k, c, t).start()
+
     @pl.loop(0, groups)
     def _(j):
         for s in range(per_group):
@@ -315,8 +352,15 @@
                 preferred_element_type=jnp.float32,
             )
             terms[c] = term.astype(jnp.bfloat16).reshape(n_t, ROWS, COLS)
-            for k in range(1, n_t):
-                term_copy(k, c, t).start()
+            start_terms(c)
+
+        @pl.when(j > 0)
+        def _():
+            for s in range(per_group):
+                start_sums((j - 1) * per_group + s)
+
+    for s in range(per_group):
+        start_sums((groups - 1) * per_group + s)
 
     for j in range(groups):
         for s in range(per_group):
@@ -324,7 +368,16 @@
             total = terms[c, t].astype(jnp.float32)
             for k in range(1, n_t):
                 source = lax.rem(t + n_t - k, n_t)
-                term_copy(k, c, source).wait_recv()
+                comes = sends(n_t - k)
+
+                @pl.when(comes)
+                def _():
+                    term_copy(k, c, source).wait_recv()
+
+                @pl.when(jnp.logical_not(comes))
+                def _():
+                    taken[source, c] = jnp.zeros((ROWS, COLS), jnp.bfloat16)
+
                 total = total + taken[source, c].astype(jnp.float32)
             branch[:, c * COLS : (c + 1) * COLS] = total.astype(jnp.bfloat16)
         for side in range(2):
@@ -417,6 +470,7 @@
             pltpu.VMEM((n_t, steps, ROWS, wide), bf16),
             pltpu.VMEM((chunks, n_t, ROWS, COLS), bf16),
             pltpu.VMEM((n_t, chunks, ROWS, COLS), bf16),
+            pltpu.VMEM((2, chunks, ROWS, COLS), bf16),
             pltpu.VMEM((ROWS, width), bf16),
             pltpu.VMEM((tokens, hidden), f32),
             pltpu.VMEM((tokens, hidden), f32),
@@ -439,6 +493,7 @@
             dma((2, steps)),
             dma((n_t - 1, chunks)),
             dma((n_t, chunks)),
+            dma((2, chunks)),
         ],
         compiler_params=pltpu.CompilerParams(
             collective_id=0, has_side_effects=True, vmem_limit_bytes=VMEM_LIMIT

time: 50.5 us -> 51.9 us (1.028)
  Pallas kernels: 48.1 us -> 49.5 us
    pallas_call x1, Pallas kernels: 48.1 us -> 49.5 us  [fused(): pl.pallas_call(functools.partial(fused_kernel, n_dp, n_t), out_shape=jax....]
where the time goes in v6:
time: 51.9 us; the launch traced here: 51.8 us
  Pallas kernels  49.5 us (95%)
  local copies, waits for them, and re-layouts  1.62 us (3%)
  between operations  0.66 us (1%)
    pallas_call x1, Pallas kernels, fused(): pl.pallas_call(functools.partial(fused_kernel, n_dp, n_t), out_shape=jax....  49.5 us
    unnamed x1, local copies, waits for them, and re-layouts  1.62 us

profile of v6, /device:TPU:1, one launch (start us, length us, event | category | flops | bytes accessed | tf_op | source)
XLA Modules:
  0.0 51.8 jit_solution(8504545198331496486)
XLA Ops:
  0.7 49.5 %shard_map.64 = bf16[24,4096]{1,0:T(8,128)(2,1)} custom-call(bf16[24,4096]{1,0:T(8,128)(2,1)} %x_ref.1, bf16[24,4096]{1,0:T(8,128)(2,1)} %g_ref.1, s32[1]{0:T(128)S(6)} %copy.8.count_ref, bf16[2064]{0:T(1024)(128)(2,1)} %bias_ref.1, bf16[2064,4096]{1,0:T(8,128)(2,1)} %up_hbm.1, bf16[2064,4096]{1,0:T(8,128)(2,1)} %down_hbm.1), custom_call_target="tpu_custom_call" | custom-call | tf_op jit(solution)/shard_map/pallas_call | solution.py:462
  50.2 1.6 %copy.9 = bf16[24,4096]{1,0:T(8,128)(2,1)} copy(bf16[24,4096]{1,0:T(8,128)(2,1)} %shard_map.64) | data formatting | bytes 393216

commit v7 on v5

--- a/solution.py
+++ b/solution.py
@@ -146,9 +146,8 @@
         cols = pl.ds(pl.multiple_of(j * wide, wide), wide)
         return pltpu.make_async_copy(source.at[:, cols], target.at[j], w_sem.at[i, j])
 
-    for i in range(2):
-        for j in range(groups):
-            weight_copy(i, j).start()
+    for j in range(groups // 2):
+        weight_copy(0, j).start()
 
     barrier = pltpu.get_barrier_semaphore()
     for k in range(1, n_dp):
@@ -200,6 +199,8 @@
     for i in range(2):
         for side in range(2):
             halo_copy(side, i).start()
+    for j in range(groups // 2, groups):
+        weight_copy(0, j).start()
     for k in range(1, n_dp):
         count_copy(k, lax.rem(me + n_dp - k, n_dp)).wait_recv()
     before = jnp.zeros(count_own.shape, jnp.int32)
@@ -275,6 +276,9 @@
             @pl.when(step + LEAD < steps)
             def _():
                 start_own(step + LEAD)
+
+            if i == 0:
+                weight_copy(1, j).start()
 
             for k in range(1, n_t):
                 source = lax.rem(t + n_t - k, n_t)

time: 50.5 us -> 50.5 us (level)
  no operation moved by 1% of the time
where the time goes in v7:
time: 50.5 us; the launch traced here: 50.4 us
  Pallas kernels  48.1 us (95%)
  local copies, waits for them, and re-layouts  1.62 us (3%)
  between operations  0.66 us (1%)
    pallas_call x1, Pallas kernels, fused(): pl.pallas_call(functools.partial(fused_kernel, n_dp, n_t), out_shape=jax....  48.1 us
    unnamed x1, local copies, waits for them, and re-layouts  1.62 us

profile of v7, /device:TPU:1, one launch (start us, length us, event | category | flops | bytes accessed | tf_op | source)
XLA Modules:
  0.0 50.4 jit_solution(16168815853732933905)
XLA Ops:
  0.7 48.1 %shard_map.64 = bf16[24,4096]{1,0:T(8,128)(2,1)} custom-call(bf16[24,4096]{1,0:T(8,128)(2,1)} %x_ref.1, bf16[24,4096]{1,0:T(8,128)(2,1)} %g_ref.1, s32[1]{0:T(128)S(6)} %copy.8.count_ref, bf16[2064]{0:T(1024)(128)(2,1)} %bias_ref.1, bf16[2064,4096]{1,0:T(8,128)(2,1)} %up_hbm.1, bf16[2064,4096]{1,0:T(8,128)(2,1)} %down_hbm.1), custom_call_target="tpu_custom_call" | custom-call | tf_op jit(solution)/shard_map/pallas_call | solution.py:413
  48.7 1.6 %copy.9 = bf16[24,4096]{1,0:T(8,128)(2,1)} copy(bf16[24,4096]{1,0:T(8,128)(2,1)} %shard_map.64) | data formatting | bytes 393216
